TPU v7x, 128 devices: a whole 4x4x4 slice. The times are simulated.
128 devices in a mesh: gx: 8 (over x, y_hi), gy: 16 (over z, y_lo, core).
Axes of the slice: x: 4, y: 4 (y_hi: 2, y_lo: 2; y = y_hi * 2 + y_lo), z: 4, core: 2. Of those that a mesh axis runs over, the one named last changes fastest.
Arguments:
- momentum_dist: float32 [19, 64, 256, 512], P(None, 'gx', 'gy'), may hold values from 0.2 to 0.8
- order_dist: float32 [19, 64, 256, 512], P(None, 'gx', 'gy'), may hold values from -0.25 to 0.25
- offsets: int32 [4], replicated, may hold values from 128 to 143, as said below
Outputs:
- next_momentum: float32 [19, 64, 256, 512], P(None, 'gx', 'gy')
- next_order: float32 [19, 64, 256, 512], P(None, 'gx', 'gy')
Inputs may be any that keep to these rules, and one draw needn't show every extreme that they name: Every offsets[k] lies from 128 to 143; offsets[0] is 128 and offsets[3] is 143.
All inputs are finite; a program needn't handle non-finite values.
Results may differ from a plain program's by a relative error of at most 0.00002.
Values sent between devices are 32-bit elements; how exact they have to be, the bound alone decides.
A program may use at most 128 MiB of HBM per device.

v0:
```python
import jax
import jax.numpy as jnp
from jax import lax
from jax.sharding import PartitionSpec as P

lattice_velocity = [
    (0, 0, 0),
    (1, 0, 0),
    (-1, 0, 0),
    (0, 1, 0),
    (0, -1, 0),
    (0, 0, 1),
    (0, 0, -1),
    (1, 1, 0),
    (-1, -1, 0),
    (1, -1, 0),
    (-1, 1, 0),
    (1, 0, 1),
    (-1, 0, -1),
    (1, 0, -1),
    (-1, 0, 1),
    (0, 1, 1),
    (0, -1, -1),
    (0, 1, -1),
    (0, -1, 1),
]
lattice_weight = [1.0 / 3.0] + [1.0 / 18.0] * 6 + [1.0 / 36.0] * 12
relax_momentum = 0.8
relax_order = 0.9
bulk_quadratic = -0.0625
bulk_quartic = 0.0625
interface_kappa = 0.04
plane_speed = 0.04
rising = [1, 7, 9, 11, 13]
falling = [2, 8, 10, 12, 14]
sideways = [3, 4, 7, 8, 9, 10, 15, 16, 17, 18]


def extended(cells, sides, width):
    for axis, dim in sides:
        count = lax.axis_size(axis)
        head = lax.slice_in_dim(cells, 0, width, axis=dim)
        tail = lax.slice_in_dim(cells, cells.shape[dim] - width, cells.shape[dim], axis=dim)
        cells = jnp.concatenate(
            [
                lax.ppermute(tail, axis, [(i, (i + 1) % count) for i in range(count)]),
                cells,
                lax.ppermute(head, axis, [((i + 1) % count, i) for i in range(count)]),
            ],
            axis=dim,
        )
    return cells


def tables(chosen):
    weight = jnp.asarray([lattice_weight[c] for c in chosen], jnp.float32).reshape(-1, 1, 1, 1)
    directions = [
        jnp.asarray([float(lattice_velocity[c][axis_place]) for c in chosen], jnp.float32).reshape(
            -1, 1, 1, 1
        )
        for axis_place in range(3)
    ]
    return (weight, directions)


def equilibria(density, order_field, potential, velocity, weight, directions):
    projection = (
        directions[0] * velocity[0] + directions[1] * velocity[1] + directions[2] * velocity[2]
    )
    speed_square = velocity[0] * velocity[0] + velocity[1] * velocity[1] + velocity[2] * velocity[2]
    shape_term = 3.0 * projection + 4.5 * projection * projection - 1.5 * speed_square
    moment_eq = weight * density * (1.0 + shape_term)
    order_eq = weight * (3.0 * potential + order_field * shape_term)
    return (moment_eq, order_eq, projection)


def collide(momentum, order, order_field, potential, gradient_parts):
    weight, directions = tables(list(range(19)))
    density = jnp.sum(momentum, axis=0)
    force_parts = [potential * part_value for part_value in gradient_parts]
    velocity = [
        (jnp.sum(directions[axis_place] * momentum, axis=0) + 0.5 * force_parts[axis_place])
        / density
        for axis_place in range(3)
    ]
    moment_eq, order_eq, projection = equilibria(
        density, order_field, potential, velocity, weight, directions
    )
    order_eq = jnp.concatenate(
        [(order_field - jnp.sum(order_eq[1:], axis=0))[None], order_eq[1:]], 0
    )
    force_projection = (
        directions[0] * force_parts[0]
        + directions[1] * force_parts[1]
        + directions[2] * force_parts[2]
    )
    velocity_force = (
        velocity[0] * force_parts[0] + velocity[1] * force_parts[1] + velocity[2] * force_parts[2]
    )
    source = (
        (1.0 - 0.5 / relax_momentum)
        * weight
        * (3.0 * (force_projection - velocity_force) + 9.0 * projection * force_projection)
    )
    moment_post = momentum - (momentum - moment_eq) / relax_momentum + source
    order_post = order - (order - order_eq) / relax_order
    return (moment_post, order_post, moment_eq, order_eq, density, velocity)


def jump_terms(
    chosen, density, order_field, potential, velocity, velocity_jump, base_moment, base_order
):
    weight, directions = tables(chosen)
    shifted_velocity = [velocity[0], velocity[1] + velocity_jump, velocity[2]]
    moment_shift, order_shift, projection = equilibria(
        density, order_field, potential, shifted_velocity, weight, directions
    )
    return (moment_shift - base_moment, order_shift - base_order)


def gather_components(values, chosen):
    return jnp.stack([values[c] for c in chosen])


def plane_windows(low_piece, up_piece, low_shift, up_shift):
    row_count = low_piece.shape[1]
    count_y = lax.axis_size("gy")
    column_slab = lax.axis_index("gy")
    plane_length = row_count * count_y
    whole_low, whole_up = (
        lax.all_gather(low_piece, "gy", axis=1, tiled=True),
        lax.all_gather(up_piece, "gy", axis=1, tiled=True),
    )

    def window_of(whole, shift_value):
        doubled = jnp.concatenate([whole, whole[:, : row_count + 3]], 1)
        first_row = jnp.mod(column_slab * row_count - 1 + shift_value, plane_length)
        return lax.dynamic_slice_in_dim(doubled, first_row, row_count + 3, 1)

    return (window_of(whole_low, low_shift), window_of(whole_up, up_shift))


def on_device(momentum_dist, order_dist, offsets):
    rows_y = momentum_dist.shape[2]
    count_x = lax.axis_size("gx")
    slab_index = lax.axis_index("gx")
    per_plane = count_x // 4
    fractions = (2.0 * jnp.arange(4, dtype=jnp.float32) + 1.0) / 8.0
    upper_slab = (slab_index + 1) % count_x
    low_mask = slab_index % per_plane == 0
    low_plane = slab_index // per_plane % 4
    up_mask = upper_slab % per_plane == 0
    up_plane = upper_slab // per_plane % 4
    low_shift = jnp.where(low_mask, offsets[low_plane], 0)
    low_near = jnp.where(low_mask, 1.0 - fractions[low_plane], 1.0)
    low_far = jnp.where(low_mask, fractions[low_plane], 0.0)
    up_shift = jnp.where(up_mask, -offsets[up_plane] - 1, 0)
    up_near = jnp.where(up_mask, fractions[up_plane], 1.0)
    up_far = jnp.where(up_mask, 1.0 - fractions[up_plane], 0.0)
    order_field = jnp.sum(order_dist, axis=0)
    rimmed = extended(order_field, (("gx", 0), ("gy", 1)), 1)
    order_low_win, order_up_win = plane_windows(
        rimmed[0:1, 1:-1], rimmed[-1:, 1:-1], low_shift, up_shift
    )
    minus_row = (
        low_near * order_low_win[:, 1 : rows_y + 1] + low_far * order_low_win[:, 2 : rows_y + 2]
    )
    plus_row = up_near * order_up_win[:, 1 : rows_y + 1] + up_far * order_up_win[:, 2 : rows_y + 2]
    order_minus = jnp.concatenate([minus_row, order_field[:-1]], 0)
    order_plus = jnp.concatenate([order_field[1:], plus_row], 0)
    order_north = rimmed[1:-1, 2:]
    order_south = rimmed[1:-1, :-2]
    order_upper = jnp.roll(order_field, -1, 2)
    order_lower = jnp.roll(order_field, 1, 2)
    laplacian = (
        order_plus
        + order_minus
        + (order_north + order_south)
        + (order_upper + order_lower)
        - 6.0 * order_field
    )
    gradient_parts = [
        0.5 * (order_plus - order_minus),
        0.5 * (order_north - order_south),
        0.5 * (order_upper - order_lower),
    ]
    potential = (
        bulk_quadratic * order_field
        + bulk_quartic * order_field * order_field * order_field
        - interface_kappa * laplacian
    )
    moment_post, order_post, moment_eq, order_eq, density, velocity = collide(
        momentum_dist, order_dist, order_field, potential, gradient_parts
    )
    top_velocity = [part_value[-1:] for part_value in velocity]
    moment_delta, order_delta = jump_terms(
        rising,
        density[-1:],
        order_field[-1:],
        potential[-1:],
        top_velocity,
        -plane_speed,
        gather_components(moment_eq, rising)[:, -1:],
        gather_components(order_eq, rising)[:, -1:],
    )
    rise_f = gather_components(moment_post, rising)[:, -1:]
    rise_g = gather_components(order_post, rising)[:, -1:]
    rise_f = jnp.where(up_mask, rise_f + moment_delta, rise_f)
    rise_g = jnp.where(up_mask, rise_g + order_delta, rise_g)
    rise_rows = jnp.concatenate([rise_f, rise_g], 0)[:, 0]
    bottom_velocity = [part_value[:1] for part_value in velocity]
    moment_delta, order_delta = jump_terms(
        falling,
        density[:1],
        order_field[:1],
        potential[:1],
        bottom_velocity,
        plane_speed,
        gather_components(moment_eq, falling)[:, :1],
        gather_components(order_eq, falling)[:, :1],
    )
    fall_f = gather_components(moment_post, falling)[:, :1]
    fall_g = gather_components(order_post, falling)[:, :1]
    fall_f = jnp.where(low_mask, fall_f + moment_delta, fall_f)
    fall_g = jnp.where(low_mask, fall_g + order_delta, fall_g)
    fall_rows = jnp.concatenate([fall_f, fall_g], 0)[:, 0]
    rise_slots = rising + [19 + c for c in rising]
    fall_slots = falling + [19 + c for c in falling]
    top_row = jnp.concatenate([moment_post[:, -1], order_post[:, -1]], 0)
    bottom_row = jnp.concatenate([moment_post[:, 0], order_post[:, 0]], 0)
    top_row = top_row.at[jnp.asarray(rise_slots)].set(rise_rows)
    bottom_row = bottom_row.at[jnp.asarray(fall_slots)].set(fall_rows)
    edge_rows = jnp.stack([bottom_row, top_row], 1)
    bordered = extended(edge_rows, (("gx", 1),), 1)
    low_piece = gather_components(bordered[:, 0], rise_slots)
    up_piece = gather_components(bordered[:, 3], fall_slots)
    low_win, up_win = plane_windows(low_piece, up_piece, low_shift, up_shift)
    side_ext = extended(
        jnp.concatenate(
            [gather_components(moment_post, sideways), gather_components(order_post, sideways)], 0
        ),
        (("gy", 2),),
        1,
    )

    def stream(post, family):
        arrived_list = []
        for component in range(19):
            step_x, step_y, step_z = lattice_velocity[component]
            if step_y != 0:
                spread = side_ext[family * 10 + sideways.index(component)]
                shifted = spread[:, 1 - step_y : 1 - step_y + rows_y]
            else:
                shifted = post[component]
            if step_x == 1:
                window = low_win[family * 5 + rising.index(component)]
                arrival = (
                    low_near * window[1 - step_y : 1 - step_y + rows_y]
                    + low_far * window[2 - step_y : 2 - step_y + rows_y]
                )
                shifted = jnp.concatenate([arrival[None], shifted[:-1]], 0)
            elif step_x == -1:
                window = up_win[family * 5 + falling.index(component)]
                arrival = (
                    up_near * window[1 - step_y : 1 - step_y + rows_y]
                    + up_far * window[2 - step_y : 2 - step_y + rows_y]
                )
                shifted = jnp.concatenate([shifted[1:], arrival[None]], 0)
            arrived_list.append(jnp.roll(shifted, step_z, 2))
        return jnp.stack(arrived_list)

    return (stream(moment_post, 0), stream(order_post, 1))


def solution(mesh):
    return jax.shard_map(
        on_device,
        mesh=mesh,
        in_specs=(P(None, "gx", "gy", None), P(None, "gx", "gy", None), P()),
        out_specs=(P(None, "gx", "gy", None), P(None, "gx", "gy", None)),
        check_vma=False,
    )
```

profile of v0, /device:TPU:1, one launch (start us, length us, event | category | flops | bytes accessed | tf_op | source)
XLA Modules:
  0.0 271.3 jit_solution(10078779065214475149)
XLA Ops:
  7.2 2.9 %reduce_sum.56 = f32[8,16,512]{2,1,0:T(8,128)S(1)} reduce(f32[19,8,16,512]{3,2,1,0:T(8,128)} %param.18, f32[]{:T(128)} %constant.137.clone.1), dimensions={0}, to_apply=%region_2.3 | reduce | flops 1179648 | bytes 5242884 | tf_op jit(solution)/shard_map/reduce_sum | solution.py:160
  10.8 5.9 %collective-permute-start = (f32[1,16,512]{2,1,0:T(8,128)S(1)}, f32[1,16,512]{2,1,0:T(8,128)S(1)}, u32[]{:S(2)}, u32[]{:S(2)}) collective-permute-start(f32[1,16,512]{2,1,0:T(8,128)S(1)} %get-tuple-element.139), channel_id=1, source_target_pairs={{16,0},{32,16},{48,32},{64,48},{80,64},{96,80},{112,96},{0,112},{1... | collective-permute-start | bytes 98312 | tf_op jit(solution)/shard_map/ppermute | solution.py:48
  17.0 2.9 %reduce_sum.54 = f32[8,16,512]{2,1,0:T(8,128)S(1)} reduce(f32[19,8,16,512]{3,2,1,0:T(8,128)} %param.17, f32[]{:T(128)} %constant.137.clone.1), dimensions={0}, to_apply=%region_0.1 | reduce | flops 1179648 | bytes 5242884 | tf_op jit(solution)/shard_map/reduce_sum | solution.py:79
  20.6 3.6 %multiply_reduce_fusion.2 = (f32[8,16,512]{2,1,0:T(8,128)S(1)}, f32[8,16,512]{2,1,0:T(8,128)S(1)}, f32[8,16,512]{2,1,0:T(8,128)S(1)}) fusion(f32[19,8,16,512]{3,2,1,0:T(8,128)} %param.17, f32[19]{0:T(128)S(1)} %copy-done.69, f32[19]{0:T(128)S(1)} %copy-done.71, f32[19]{0:T(128)S(1)} %copy-done.70), kind=kLoop, calls=%fused_computation.17 | loop fusion | flops 7274496 | bytes 5767396 | tf_op jit(solution)/shard_map/reduce_sum | solution.py:82
  29.6 23.2 %all_gather.12 = f32[1,256,512]{2,1,0:T(8,128)S(1)} all-gather(f32[1,16,512]{2,1,0:T(8,128)S(1)} %collective-permute-done), channel_id=1, replica_groups=mesh['gx'=8,'gy'=16] {'gy'}, dimensions={1}, use_global_device_ids=true | all-gather | bytes 557056 | tf_op jit(solution)/shard_map/all_gather | solution.py:132
  52.9 18.6 %all_gather.13 = f32[1,256,512]{2,1,0:T(8,128)S(1)} all-gather(f32[1,16,512]{2,1,0:T(8,128)S(1)} %collective-permute-done.1), channel_id=1, replica_groups=mesh['gx'=8,'gy'=16] {'gy'}, dimensions={1}, use_global_device_ids=true | all-gather | bytes 557056 | tf_op jit(solution)/shard_map/all_gather | solution.py:131
  71.7 1.6 collective-permute-start.3
  73.4 1.3 collective-permute-done.2
  75.6 7.0 %add_multiply_fusion.1 = (f32[19,8,16,512]{3,2,0,1:T(8,128)}, f32[19,8,16,512]{3,2,0,1:T(8,128)S(1)}, f32[19,8,16,512]{3,2,0,1:T(8,128)S(1)}) fusion(f32[8,16,512]{2,1,0:T(8,128)S(1)} %get-tuple-element.7, f32[8,16,512]{2,1,0:T(8,128)S(1)} %get-tuple-element.12, f32[19]{0:T(128)S(1)} %copy-done.71, f32[8,16,512]{2,1,0:T(8,128)S(1)} %get-tuple-element.10, ...), kind=kLoop, calls=%fused_computation.13 | loop fusion | flops 37355520 | bytes 22806908 | tf_op jit(solution)/shard_map/mul | solution.py:72
  82.6 0.9 slice_dynamic-update-slice_fusion.10
  83.5 2.9 %slice_reduce_fusion = (f32[8,16,512]{2,1,0:T(8,128)S(1)}, f32[18,8,16,512]{3,2,0,1:T(8,128)}) fusion(f32[19,8,16,512]{3,2,0,1:T(8,128)S(1)} %get-tuple-element.99), kind=kLoop, calls=%fused_computation.378 | loop fusion | flops 1114112 | bytes 9699328 | tf_op jit(solution)/shard_map/reduce_sum | solution.py:90
  87.8 0.8 slice-done.3
  88.6 3.8 %fusion.1 = f32[19,8,16,512]{3,2,0,1:T(8,128)S(1)} fusion(f32[18,8,16,512]{3,2,0,1:T(8,128)} %get-tuple-element.96, f32[1,8,16,512]{3,2,0,1:T(8,128)S(1)} %subtract_bitcast_fusion, f32[19,8,16,512]{3,2,1,0:T(8,128)S(1)} %bitcast.412), kind=kLoop, calls=%fused_computation.9 | loop fusion | flops 4980736 | bytes 14942208 | tf_op jit(solution)/shard_map/sub | solution.py:106
  92.9 1.8 copy-done.42
  94.7 1.2 copy-done.43
  96.8 1.1 slice_bitcast_fusion.24
  98.3 0.7 maximum_bitcast_fusion.1
  99.9 1.9 scatter_fusion.1
  101.8 6.0 %collective-permute-start.5 = (f32[38,1,16,512]{3,2,0,1:T(8,128)S(1)}, f32[38,1,16,512]{3,2,0,1:T(8,128)S(1)}, u32[]{:S(2)}, u32[]{:S(2)}) collective-permute-start(f32[38,1,16,512]{3,2,0,1:T(8,128)S(1)} %bitcast.416), channel_id=1, source_target_pairs={{16,0},{32,16},{48,32},{64,48},{80,64},{96,80},{112,96},{0,112},{1... | collective-permute-start | bytes 3735560 | tf_op jit(solution)/shard_map/ppermute | solution.py:48
  107.9 22.4 %collective-permute-done.5 = f32[38,1,16,512]{3,2,0,1:T(8,128)S(1)} collective-permute-done((f32[38,1,16,512]{3,2,0,1:T(8,128)S(1)}, f32[38,1,16,512]{3,2,0,1:T(8,128)S(1)}, u32[]{:S(2)}, u32[]{:S(2)}) %collective-permute-start.5) | collective-permute-done | bytes 1245216 | tf_op jit(solution)/shard_map/ppermute | solution.py:48
  131.3 1.4 add_select_fusion.3
  132.7 1.0 scatter_fusion
  133.7 1.3 collective-permute-start.4
  134.9 32.6 %collective-permute-done.4 = f32[38,1,16,512]{3,2,1,0:T(8,128)S(1)} collective-permute-done((f32[38,1,16,512]{3,2,1,0:T(8,128)S(1)}, f32[38,1,16,512]{3,2,1,0:T(8,128)S(1)}, u32[]{:S(2)}, u32[]{:S(2)}) %collective-permute-start.4) | collective-permute-done | bytes 1245216 | tf_op jit(solution)/shard_map/ppermute | solution.py:46
  168.4 1.2 slice_dynamic-update-slice_fusion.5
  169.7 1.7 slice_dynamic-update-slice_fusion.3
  171.4 1.3 slice_dynamic-update-slice_fusion.2
  173.7 23.3 %collective-permute-start.6 = (f32[20,8,1,512]{3,2,0,1:T(1,128)S(1)}, f32[20,8,1,512]{3,2,0,1:T(1,128)S(1)}, u32[]{:S(2)}, u32[]{:S(2)}) collective-permute-start(f32[20,8,1,512]{3,2,0,1:T(1,128)S(1)} %get-tuple-element.33), channel_id=1, source_target_pairs={{0,1},{1,2},{2,3},{3,4},{4,5},{5,6},{6,7},{7,8},{8,9},{9,10},{10,1... | collective-permute-start | bytes 983048 | tf_op jit(solution)/shard_map/ppermute | solution.py:46
  197.7 1.0 slice_bitcast_fusion.34
  198.6 1.7 fusion.36
  200.3 0.8 slice.1478
  201.2 0.8 slice.1417
  203.4 2.4 slice_bitcast_fusion.40
  205.9 1.6 pad_maximum_fusion
  207.5 2.1 slice_bitcast_fusion.4
  209.5 0.7 slice.1514
  211.0 0.8 slice.1516
  212.5 0.8 slice.1519
  213.9 0.8 slice.1523
  215.4 0.7 slice.1453
  216.8 0.9 slice.1455
  218.3 0.8 slice.1458
  220.7 0.7 slice.1485
  221.4 0.7 slice.1491
  223.5 0.7 slice.1424
  225.8 1.1 slice.1398
  226.9 1.3 fusion.2
  229.5 11.1 %all-gather.3.cloned.1.call-done = f32[10,256,512]{2,1,0:T(8,128)} async-done(((f32[10,16,512]{2,1,0:T(8,128)}), f32[10,256,512]{2,1,0:T(8,128)}) %all-gather.3.cloned.1.call-update) | async-done | bytes 5242896 | tf_op jit(solution)/shard_map/all_gather | solution.py:131
  240.6 1.1 slice.1352
  241.8 1.4 fusion.3
  243.4 2.1 fusion.49
  245.5 1.7 fusion.50
  248.0 0.7 fusion.19
  248.8 0.8 fusion.51
  249.7 0.8 fusion.52
  253.4 0.9 fusion.18
  254.2 0.8 fusion.15
  255.2 0.8 fusion.12
  257.4 0.9 fusion.9
  258.2 0.8 fusion.57
  259.1 0.8 fusion.58
  259.9 0.8 fusion.59
  260.7 0.8 fusion.60
  262.2 2.3 copy-done.67
  (307 shorter events, 27.9 us)
Async XLA Ops:
  7.2 218.6 %all-gather.5.cloned.1.call-start = ((), (), s32[]{:S(2)}) async-start(), calls=%async_computation.1 | async-start | bytes 5570560 | tf_op jit(solution)/shard_map/all_gather | solution.py:132
  10.1 10.5 %copy-start.69 = (f32[19]{0:T(128)S(1)}, f32[19]{0:T(128)}, u32[]{:S(2)}) copy-start(f32[19]{0:T(128)} %constant.172.clone) | copy-start | bytes 232
  10.2 10.5 %copy-start.70 = (f32[19]{0:T(128)S(1)}, f32[19]{0:T(128)}, u32[]{:S(2)}) copy-start(f32[19]{0:T(128)} %constant.173.clone) | copy-start | bytes 232
  10.2 10.4 %copy-start.71 = (f32[19]{0:T(128)S(1)}, f32[19]{0:T(128)}, u32[]{:S(2)}) copy-start(f32[19]{0:T(128)} %constant.174.clone) | copy-start | bytes 232
  10.8 18.8 %collective-permute-start = (f32[1,16,512]{2,1,0:T(8,128)S(1)}, f32[1,16,512]{2,1,0:T(8,128)S(1)}, u32[]{:S(2)}, u32[]{:S(2)}) collective-permute-start(f32[1,16,512]{2,1,0:T(8,128)S(1)} %get-tuple-element.139), channel_id=1, source_target_pairs={{16,0},{32,16},{48,32},{64,48},{80,64},{96,80},{112,96},{0,112},{1... | collective-permute-start | bytes 98312 | tf_op jit(solution)/shard_map/ppermute | solution.py:48
  16.8 36.1 %collective-permute-start.1 = (f32[1,16,512]{2,1,0:T(8,128)S(1)}, f32[1,16,512]{2,1,0:T(8,128)S(1)}, u32[]{:S(2)}, u32[]{:S(2)}) collective-permute-start(f32[1,16,512]{2,1,0:T(8,128)S(1)} %get-tuple-element.138), channel_id=1, source_target_pairs={{0,16},{16,32},{32,48},{48,64},{64,80},{80,96},{96,112},{112,0},{1... | collective-permute-start | bytes 98312 | tf_op jit(solution)/shard_map/ppermute | solution.py:46
  17.0 9.3 %copy-start.72 = (s32[4]{0:T(128)S(1)}, s32[4]{0:T(128)}, u32[]{:S(2)}) copy-start(s32[4]{0:T(128)} %param.19) | copy-start | bytes 52
  20.6 55.0 %slice-start = ((s8[4980736]{0:T(1024)(128)(4,1)}), s8[786432]{0:T(1024)(128)(4,1)S(1)}, s32[]{:S(2)}) async-start(s8[4980736]{0:T(1024)(128)(4,1)} %bitcast.409), calls=%async_computation.2 | async-start | bytes 1572864
  71.4 3.3 %collective-permute-start.2 = (f32[10,1,512]{2,1,0:T(1,128)S(1)}, f32[10,1,512]{2,1,0:T(1,128)S(1)}, u32[]{:S(2)}, u32[]{:S(2)}) collective-permute-start(f32[10,1,512]{2,1,0:T(1,128)S(1)} %get-tuple-element.122), channel_id=1, source_target_pairs={{1,0},{2,1},{3,2},{4,3},{5,4},{6,5},{7,6},{8,7},{9,8},{10,9},{11,1... | collective-permute-start | bytes 61448 | tf_op jit(solution)/shard_map/ppermute | solution.py:48
  71.7 3.0 %collective-permute-start.3 = (f32[10,1,512]{2,1,0:T(1,128)S(1)}, f32[10,1,512]{2,1,0:T(1,128)S(1)}, u32[]{:S(2)}, u32[]{:S(2)}) collective-permute-start(f32[10,1,512]{2,1,0:T(1,128)S(1)} %get-tuple-element.123), channel_id=1, source_target_pairs={{0,1},{1,2},{2,3},{3,4},{4,5},{5,6},{6,7},{7,8},{8,9},{9,10},{10,1... | collective-permute-start | bytes 61448 | tf_op jit(solution)/shard_map/ppermute | solution.py:46
  82.6 14.0 %copy-start = (f32[19,8,16,512]{3,2,0,1:T(8,128)}, f32[19,8,16,512]{3,2,0,1:T(8,128)S(1)}, u32[]{:S(2)}) copy-start(f32[19,8,16,512]{3,2,0,1:T(8,128)S(1)} %get-tuple-element.98) | copy-start | bytes 14942212
  82.6 5.2 %slice-start.2 = ((s8[4980736]{0:T(1024)(128)(4,1)}), s8[4194304]{0:T(1024)(128)(4,1)S(1)}, s32[]{:S(2)}) async-start(s8[4980736]{0:T(1024)(128)(4,1)} %bitcast.411), calls=%async_computation.4 | async-start | bytes 8388608
  83.5 5.1 %slice-start.3 = ((s8[4980736]{0:T(1024)(128)(4,1)}), s8[786432]{0:T(1024)(128)(4,1)S(1)}, s32[]{:S(2)}) async-start(s8[4980736]{0:T(1024)(128)(4,1)} %bitcast.411), calls=%async_computation.5 | async-start | bytes 1572864
  87.1 5.7 %slice-start.4 = ((s8[4980736]{0:T(1024)(128)(4,1)}), s8[786432]{0:T(1024)(128)(4,1)S(1)}, s32[]{:S(2)}) async-start(s8[4980736]{0:T(1024)(128)(4,1)} %bitcast.413), calls=%async_computation.6 | async-start | bytes 1572864
  92.4 7.6 %copy-start.1 = (f32[19,8,16,512]{3,2,0,1:T(8,128)}, f32[19,8,16,512]{3,2,0,1:T(8,128)S(1)}, u32[]{:S(2)}) copy-start(f32[19,8,16,512]{3,2,0,1:T(8,128)S(1)} %fusion.1) | copy-start | bytes 14942212
  97.9 33.3 %copy-start.47 = (f32[16,512]{1,0:T(8,128)S(1)}, f32[16,512]{1,0:T(8,128)}, u32[]{:S(2)}) copy-start(f32[16,512]{1,0:T(8,128)} %get-tuple-element.161) | copy-start | bytes 98308
  97.9 33.3 %copy-start.48 = (f32[16,512]{1,0:T(8,128)S(1)}, f32[16,512]{1,0:T(8,128)}, u32[]{:S(2)}) copy-start(f32[16,512]{1,0:T(8,128)} %get-tuple-element.165) | copy-start | bytes 98308
  97.9 33.3 %copy-start.49 = (f32[16,512]{1,0:T(8,128)S(1)}, f32[16,512]{1,0:T(8,128)}, u32[]{:S(2)}) copy-start(f32[16,512]{1,0:T(8,128)} %get-tuple-element.166) | copy-start | bytes 98308
  98.0 33.3 %copy-start.61 = (f32[16,512]{1,0:T(8,128)S(1)}, f32[16,512]{1,0:T(8,128)}, u32[]{:S(2)}) copy-start(f32[16,512]{1,0:T(8,128)} %get-tuple-element.137) | copy-start | bytes 98308
  98.0 33.3 %copy-start.62 = (f32[16,512]{1,0:T(8,128)S(1)}, f32[16,512]{1,0:T(8,128)}, u32[]{:S(2)}) copy-start(f32[16,512]{1,0:T(8,128)} %get-tuple-element.125) | copy-start | bytes 98308
  98.0 33.3 %copy-start.75 = (f32[5]{0:T(128)S(1)}, f32[5]{0:T(128)}, u32[]{:S(2)}) copy-start(f32[5]{0:T(128)} %constant.177.clone) | copy-start | bytes 64
  98.0 33.3 %copy-start.76 = (f32[5]{0:T(128)S(1)}, f32[5]{0:T(128)}, u32[]{:S(2)}) copy-start(f32[5]{0:T(128)} %constant.178.clone) | copy-start | bytes 64
  98.3 34.4 %copy-start.73 = (s32[10]{0:T(128)S(1)}, s32[10]{0:T(128)}, u32[]{:S(2)}) copy-start(s32[10]{0:T(128)} %constant.193) | copy-start | bytes 124
  101.8 28.5 %collective-permute-start.5 = (f32[38,1,16,512]{3,2,0,1:T(8,128)S(1)}, f32[38,1,16,512]{3,2,0,1:T(8,128)S(1)}, u32[]{:S(2)}, u32[]{:S(2)}) collective-permute-start(f32[38,1,16,512]{3,2,0,1:T(8,128)S(1)} %bitcast.416), channel_id=1, source_target_pairs={{16,0},{32,16},{48,32},{64,48},{80,64},{96,80},{112,96},{0,112},{1... | collective-permute-start | bytes 3735560 | tf_op jit(solution)/shard_map/ppermute | solution.py:48
  131.2 109.5 %all-gather.3.cloned.1.call-start = ((), (), s32[]{:S(2)}) async-start(), calls=%async_computation | async-start | bytes 5570560 | tf_op jit(solution)/shard_map/all_gather | solution.py:131
  133.7 33.9 %collective-permute-start.4 = (f32[38,1,16,512]{3,2,1,0:T(8,128)S(1)}, f32[38,1,16,512]{3,2,1,0:T(8,128)S(1)}, u32[]{:S(2)}, u32[]{:S(2)}) collective-permute-start(f32[38,1,16,512]{3,2,1,0:T(8,128)S(1)} %bitcast.415), channel_id=1, source_target_pairs={{0,16},{16,32},{32,48},{48,64},{64,80},{80,96},{96,112},{112,0},{1... | collective-permute-start | bytes 3735560 | tf_op jit(solution)/shard_map/ppermute | solution.py:46
  172.7 27.6 %copy-start.3 = (f32[8,16,512]{2,1,0:T(8,128)S(1)}, f32[8,16,512]{2,1,0:T(8,128)}, u32[]{:S(2)}) copy-start(f32[8,16,512]{2,1,0:T(8,128)} %get-tuple-element.41) | copy-start | bytes 786436
  173.7 32.2 %collective-permute-start.6 = (f32[20,8,1,512]{3,2,0,1:T(1,128)S(1)}, f32[20,8,1,512]{3,2,0,1:T(1,128)S(1)}, u32[]{:S(2)}, u32[]{:S(2)}) collective-permute-start(f32[20,8,1,512]{3,2,0,1:T(1,128)S(1)} %get-tuple-element.33), channel_id=1, source_target_pairs={{0,1},{1,2},{2,3},{3,4},{4,5},{5,6},{6,7},{7,8},{8,9},{9,10},{10,1... | collective-permute-start | bytes 983048 | tf_op jit(solution)/shard_map/ppermute | solution.py:46
  196.9 8.9 %collective-permute-start.7 = (f32[20,8,1,512]{3,2,0,1:T(1,128)S(1)}, f32[20,8,1,512]{3,2,0,1:T(1,128)S(1)}, u32[]{:S(2)}, u32[]{:S(2)}) collective-permute-start(f32[20,8,1,512]{3,2,0,1:T(1,128)S(1)} %get-tuple-element.34), channel_id=1, source_target_pairs={{1,0},{2,1},{3,2},{4,3},{5,4},{6,5},{7,6},{8,7},{9,8},{10,9},{11,1... | collective-permute-start | bytes 983048 | tf_op jit(solution)/shard_map/ppermute | solution.py:48
  228.8 18.5 %copy-start.6 = (f32[8,18,512]{2,1,0:T(8,128)S(1)}, f32[8,18,512]{2,1,0:T(8,128)}, u32[]{:S(2)}) copy-start(f32[8,18,512]{2,1,0:T(8,128)} %get-tuple-element.23) | copy-start | bytes 884740
  229.5 18.5 %copy-start.5 = (f32[8,18,512]{2,1,0:T(8,128)S(1)}, f32[8,18,512]{2,1,0:T(8,128)}, u32[]{:S(2)}) copy-start(f32[8,18,512]{2,1,0:T(8,128)} %get-tuple-element.22) | copy-start | bytes 884740
  240.6 4.8 %copy-start.60 = (f32[1,16,512]{2,1,0:T(8,128)S(1)}, f32[1,16,512]{2,1,0:T(8,128)}, u32[]{:S(2)}) copy-start(f32[1,16,512]{2,1,0:T(8,128)} %get-tuple-element.107) | copy-start | bytes 98308
  241.7 8.0 %copy-start.15 = (f32[8,16,511]{2,1,0:T(8,128)S(1)}, f32[8,16,511]{2,1,0:T(8,128)}, u32[]{:S(2)}) copy-start(f32[8,16,511]{2,1,0:T(8,128)} %slice.1478) | copy-start | bytes 784900
  241.7 8.8 %copy-start.23 = (f32[7,16,512]{2,1,0:T(8,128)S(1)}, f32[7,16,512]{2,1,0:T(8,128)}, u32[]{:S(2)}) copy-start(f32[7,16,512]{2,1,0:T(8,128)} %slice.1483) | copy-start | bytes 688132
  241.7 9.5 %copy-start.22 = (f32[7,16,512]{2,1,0:T(8,128)S(1)}, f32[7,16,512]{2,1,0:T(8,128)}, u32[]{:S(2)}) copy-start(f32[7,16,512]{2,1,0:T(8,128)} %slice.1485) | copy-start | bytes 688132
  241.7 9.5 %copy-start.59 = (f32[1,16,512]{2,1,0:T(8,128)S(1)}, f32[1,16,512]{2,1,0:T(8,128)}, u32[]{:S(2)}) copy-start(f32[1,16,512]{2,1,0:T(8,128)} %get-tuple-element.103) | copy-start | bytes 98308
  241.8 10.2 %copy-start.21 = (f32[7,16,512]{2,1,0:T(8,128)S(1)}, f32[7,16,512]{2,1,0:T(8,128)}, u32[]{:S(2)}) copy-start(f32[7,16,512]{2,1,0:T(8,128)} %slice.1491) | copy-start | bytes 688132
  241.8 10.9 %copy-start.20 = (f32[7,16,512]{2,1,0:T(8,128)S(1)}, f32[7,16,512]{2,1,0:T(8,128)}, u32[]{:S(2)}) copy-start(f32[7,16,512]{2,1,0:T(8,128)} %slice.1493) | copy-start | bytes 688132
  241.8 10.9 %copy-start.58 = (f32[1,16,512]{2,1,0:T(8,128)S(1)}, f32[1,16,512]{2,1,0:T(8,128)}, u32[]{:S(2)}) copy-start(f32[1,16,512]{2,1,0:T(8,128)} %get-tuple-element.105) | copy-start | bytes 98308
  241.8 14.2 %slice-start.6 = ((s8[4980736]{0:T(1024)(128)(4,1)}), s8[4194304]{0:T(1024)(128)(4,1)S(1)}, s32[]{:S(2)}) async-start(s8[4980736]{0:T(1024)(128)(4,1)} %bitcast.428), calls=%async_computation.8 | async-start | bytes 8388608
  243.2 10.2 %copy-start.28 = (f32[7,16,512]{2,1,0:T(8,128)S(1)}, f32[7,16,512]{2,1,0:T(8,128)}, u32[]{:S(2)}) copy-start(f32[7,16,512]{2,1,0:T(8,128)} %get-tuple-element.38) | copy-start | bytes 688132
  243.2 12.8 %copy-start.29 = (f32[7,16,512]{2,1,0:T(8,128)S(1)}, f32[7,16,512]{2,1,0:T(8,128)}, u32[]{:S(2)}) copy-start(f32[7,16,512]{2,1,0:T(8,128)} %get-tuple-element.49) | copy-start | bytes 688132
  243.2 12.8 %copy-start.27 = (f32[7,16,512]{2,1,0:T(8,128)S(1)}, f32[7,16,512]{2,1,0:T(8,128)}, u32[]{:S(2)}) copy-start(f32[7,16,512]{2,1,0:T(8,128)} %get-tuple-element.48) | copy-start | bytes 688132
  243.2 12.8 %copy-start.66 = (f32[1,16,512]{2,1,0:T(8,128)S(1)}, f32[1,16,512]{2,1,0:T(8,128)}, u32[]{:S(2)}) copy-start(f32[1,16,512]{2,1,0:T(8,128)} %get-tuple-element.119) | copy-start | bytes 98308
  243.4 12.8 %copy-start.4 = (f32[8,18,512]{2,1,0:T(8,128)S(1)}, f32[8,18,512]{2,1,0:T(8,128)}, u32[]{:S(2)}) copy-start(f32[8,18,512]{2,1,0:T(8,128)} %get-tuple-element.32) | copy-start | bytes 884740
  245.5 10.5 %slice-start.7 = ((s8[4980736]{0:T(1024)(128)(4,1)}), s8[786432]{0:T(1024)(128)(4,1)S(1)}, s32[]{:S(2)}) async-start(s8[4980736]{0:T(1024)(128)(4,1)} %bitcast.428), calls=%async_computation.9 | async-start | bytes 1572864
  247.2 9.2 %copy-start.40 = (f32[8,16,1]{2,1,0:T(8,128)S(1)}, f32[8,16,1]{2,1,0:T(8,128)}, u32[]{:S(2)}) copy-start(f32[8,16,1]{2,1,0:T(8,128)} %slice.1414) | copy-start | bytes 1540
  247.9 8.6 %copy-start.10 = (f32[8,16,511]{2,1,0:T(8,128)S(1)}, f32[8,16,511]{2,1,0:T(8,128)}, u32[]{:S(2)}) copy-start(f32[8,16,511]{2,1,0:T(8,128)} %slice.1417) | copy-start | bytes 784900
  247.9 8.6 %copy-start.35 = (f32[8,16,1]{2,1,0:T(8,128)S(1)}, f32[8,16,1]{2,1,0:T(8,128)}, u32[]{:S(2)}) copy-start(f32[8,16,1]{2,1,0:T(8,128)} %slice.1418) | copy-start | bytes 1540
  248.8 7.9 %copy-start.19 = (f32[7,16,512]{2,1,0:T(8,128)S(1)}, f32[7,16,512]{2,1,0:T(8,128)}, u32[]{:S(2)}) copy-start(f32[7,16,512]{2,1,0:T(8,128)} %slice.1422) | copy-start | bytes 688132
  249.7 7.1 %copy-start.18 = (f32[7,16,512]{2,1,0:T(8,128)S(1)}, f32[7,16,512]{2,1,0:T(8,128)}, u32[]{:S(2)}) copy-start(f32[7,16,512]{2,1,0:T(8,128)} %slice.1424) | copy-start | bytes 688132
  249.7 7.1 %copy-start.57 = (f32[1,16,512]{2,1,0:T(8,128)S(1)}, f32[1,16,512]{2,1,0:T(8,128)}, u32[]{:S(2)}) copy-start(f32[1,16,512]{2,1,0:T(8,128)} %get-tuple-element.108) | copy-start | bytes 98308
  249.7 7.1 %copy-start.17 = (f32[7,16,512]{2,1,0:T(8,128)S(1)}, f32[7,16,512]{2,1,0:T(8,128)}, u32[]{:S(2)}) copy-start(f32[7,16,512]{2,1,0:T(8,128)} %slice.1430) | copy-start | bytes 688132
  250.5 6.3 %copy-start.16 = (f32[7,16,512]{2,1,0:T(8,128)S(1)}, f32[7,16,512]{2,1,0:T(8,128)}, u32[]{:S(2)}) copy-start(f32[7,16,512]{2,1,0:T(8,128)} %slice.1432) | copy-start | bytes 688132
  250.5 6.3 %copy-start.56 = (f32[1,16,512]{2,1,0:T(8,128)S(1)}, f32[1,16,512]{2,1,0:T(8,128)}, u32[]{:S(2)}) copy-start(f32[1,16,512]{2,1,0:T(8,128)} %get-tuple-element.106) | copy-start | bytes 98308
  251.2 5.7 %copy-start.26 = (f32[7,16,512]{2,1,0:T(8,128)S(1)}, f32[7,16,512]{2,1,0:T(8,128)}, u32[]{:S(2)}) copy-start(f32[7,16,512]{2,1,0:T(8,128)} %get-tuple-element.47) | copy-start | bytes 688132
  256.2 5.3 %copy-start.24 = (f32[7,16,512]{2,1,0:T(8,128)S(1)}, f32[7,16,512]{2,1,0:T(8,128)}, u32[]{:S(2)}) copy-start(f32[7,16,512]{2,1,0:T(8,128)} %get-tuple-element.45) | copy-start | bytes 688132
  256.2 5.3 %copy-start.65 = (f32[1,16,512]{2,1,0:T(8,128)S(1)}, f32[1,16,512]{2,1,0:T(8,128)}, u32[]{:S(2)}) copy-start(f32[1,16,512]{2,1,0:T(8,128)} %get-tuple-element.118) | copy-start | bytes 98308
  256.2 5.4 %copy-start.9 = (f32[8,16,511]{2,1,0:T(8,128)S(1)}, f32[8,16,511]{2,1,0:T(8,128)}, u32[]{:S(2)}) copy-start(f32[8,16,511]{2,1,0:T(8,128)} %slice.1453) | copy-start | bytes 784900
  256.3 5.4 %copy-start.34 = (f32[8,16,1]{2,1,0:T(8,128)S(1)}, f32[8,16,1]{2,1,0:T(8,128)}, u32[]{:S(2)}) copy-start(f32[8,16,1]{2,1,0:T(8,128)} %slice.1452) | copy-start | bytes 1540
  256.4 5.4 %copy-start.8 = (f32[8,16,511]{2,1,0:T(8,128)S(1)}, f32[8,16,511]{2,1,0:T(8,128)}, u32[]{:S(2)}) copy-start(f32[8,16,511]{2,1,0:T(8,128)} %slice.1455) | copy-start | bytes 784900
  256.4 5.4 %copy-start.33 = (f32[8,16,1]{2,1,0:T(8,128)S(1)}, f32[8,16,1]{2,1,0:T(8,128)}, u32[]{:S(2)}) copy-start(f32[8,16,1]{2,1,0:T(8,128)} %slice.1456) | copy-start | bytes 1540
  256.6 5.4 %copy-start.7 = (f32[8,16,511]{2,1,0:T(8,128)S(1)}, f32[8,16,511]{2,1,0:T(8,128)}, u32[]{:S(2)}) copy-start(f32[8,16,511]{2,1,0:T(8,128)} %slice.1458) | copy-start | bytes 784900
  256.6 5.4 %copy-start.32 = (f32[8,16,1]{2,1,0:T(8,128)S(1)}, f32[8,16,1]{2,1,0:T(8,128)}, u32[]{:S(2)}) copy-start(f32[8,16,1]{2,1,0:T(8,128)} %slice.1459) | copy-start | bytes 1540
  (35 other events, 89.8 us)
Sparse Core Ops, SparseCore 0:
  131.3 63.7 all-gather.4
  196.8 43.7 all-gather.2
where the time goes:
time: 272 us; the launch traced here: 271 us
  waiting for transfers between devices  67.6 us (25%)
  local copies, waits for them, and re-layouts  53.7 us (20%)
  other arithmetic  50 us (18%)
  blocking collectives  41.7 us (15%)
  starting transfers between devices  38.4 us (14%)
  between operations  19.8 us (7%)
    ppermute x4, waiting for transfers between devices, extended(): lax.ppermute(tail, axis, [(i, (i + 1) % count) for i in range(count)])  32.6 us
    ppermute x4, starting transfers between devices, extended(): lax.ppermute(tail, axis, [(i, (i + 1) % count) for i in range(count)])  26.1 us
    ppermute x4, waiting for transfers between devices, extended(): lax.ppermute(head, axis, [((i + 1) % count, i) for i in range(count)])  23.8 us
    all_gather x1, blocking collectives, plane_windows(): lax.all_gather(up_piece, 'gy', axis=1, tiled=True)  23.2 us
    unnamed x223, local copies, waits for them, and re-layouts  18.9 us
    all_gather x1, blocking collectives, plane_windows(): lax.all_gather(low_piece, 'gy', axis=1, tiled=True)  18.6 us
    unnamed x34, other arithmetic  15.2 us
    slice x22, local copies, waits for them, and re-layouts, stream(): arrived_list.append(jnp.roll(shifted, step_z, 2))  13.5 us
  transfers between devices with their start and end apart: 10, of which 4 were waited for; matrix products, arithmetic and copies ran while one was open for 18% of the time, Pallas kernels for 0%

commit v1 on v0

v1 whole, which is shorter than its diff:
```python
import jax
import jax.numpy as jnp
from jax import lax
from jax.experimental import pallas as pl
from jax.experimental.pallas import tpu as pltpu
from jax.sharding import PartitionSpec as P

lattice_velocity = [
    (0, 0, 0),
    (1, 0, 0),
    (-1, 0, 0),
    (0, 1, 0),
    (0, -1, 0),
    (0, 0, 1),
    (0, 0, -1),
    (1, 1, 0),
    (-1, -1, 0),
    (1, -1, 0),
    (-1, 1, 0),
    (1, 0, 1),
    (-1, 0, -1),
    (1, 0, -1),
    (-1, 0, 1),
    (0, 1, 1),
    (0, -1, -1),
    (0, 1, -1),
    (0, -1, 1),
]
plane_speed = 0.04
rising = [1, 7, 9, 11, 13]
northward = [3, 7, 10, 15, 17]
southward = [4, 8, 9, 16, 18]
level = [c for c in range(19) if lattice_velocity[c][0] == 0]
pairs = [1, 3, 5, 7, 9, 11, 13, 15, 17]
QX, QY, QZ = 8, 16, 512
NGX, NGY = 8, 16
MESH = pl.DeviceIdType.MESH


def axis_sum(direction, parts):
    total = None
    for sign, part in zip(direction, parts):
        if sign == 0:
            continue
        if total is None:
            total = part if sign > 0 else -part
        else:
            total = total + part if sign > 0 else total - part
    return total


def streamed(v, step_y, step_z):
    if step_z:
        v = pltpu.roll(v, step_z % QZ, 1)
    if step_y:
        v = pltpu.roll(v, step_y % QY, 0)
    return v


def step_kernel(
    off_ref, f_hbm, g_hbm, fo, go,
    fin, gin, ph, wp, yps, yp, mm, sb, ob, oc, wb, we, ce, ys, yr,
    load_sem, send_sem, recv_sem,
):
    gx, gy = lax.axis_index("gx"), lax.axis_index("gy")
    odd = lax.rem(gx, 2)
    is_odd = odd == 1
    flat_gx = gx + 1 - 2 * odd
    plane_gx = lax.rem(gx + 2 * odd + NGX - 1, NGX)
    ring = lambda v: lax.rem(v + 2 * NGY, NGY)
    north, south = ring(gy + 1), ring(gy - 1)
    to_a, to_b = ring(gy + 9 - 17 * odd), ring(gy + 8 - 17 * odd)
    to_hi, to_lo = ring(gy + 10 - 17 * odd), ring(gy + 7 - 17 * odd)
    partners = [
        (gx, north), (gx, south),
        (flat_gx, gy), (flat_gx, north), (flat_gx, south),
        (plane_gx, to_a), (plane_gx, to_b), (plane_gx, to_hi), (plane_gx, to_lo),
    ]
    barrier = pltpu.get_barrier_semaphore()
    for partner in partners:
        pl.semaphore_signal(barrier, inc=1, device_id=partner, device_id_type=MESH)

    def load(which, x):
        source, target = ((g_hbm, gin), (f_hbm, fin))[which]
        return pltpu.make_async_copy(source.at[:, x], target.at[:, x], load_sem.at[which, x])

    for which in range(2):
        for x in range(QX):
            load(which, x).start()

    def remote(k, source, target, device):
        return pltpu.make_async_remote_copy(
            src_ref=source, dst_ref=target, send_sem=send_sem.at[k], recv_sem=recv_sem.at[k],
            device_id=device, device_id_type=MESH,
        )

    def phi_row(x, carry):
        load(0, x).wait()
        total = gin[0, x]
        for c in range(1, 19):
            total = total + gin[c, x]
        ph[x + 1] = total
        yps[0, pl.ds(x, 1), :] = total[QY - 1 : QY]
        yps[1, pl.ds(x, 1), :] = total[0:1]
        return carry

    lax.fori_loop(0, QX, phi_row, 0)

    flat_x, plane_x = 7 - 7 * odd, 7 * odd
    phi_copies = [
        remote(0, ph.at[flat_x + 1], ph.at[9 * odd], (flat_gx, gy)),
        remote(1, ph.at[plane_x + 1], wp.at[pl.ds(0, QY)], (plane_gx, to_a)),
        remote(2, ph.at[plane_x + 1], wp.at[pl.ds(QY, QY)], (plane_gx, to_b)),
        remote(3, yps.at[0], yp.at[0], (gx, north)),
        remote(4, yps.at[1], yp.at[1], (gx, south)),
    ]
    pl.semaphore_wait(barrier, len(partners))
    for copy in phi_copies:
        copy.start()

    plane = lax.rem((gx + odd) // 2, 4)
    fraction = (2 * plane + 1).astype(jnp.float32) * 0.125
    near = jnp.where(is_odd, fraction, 1.0 - fraction)
    far = 1.0 - near
    rest = off_ref[plane] - 8 * QY
    first = jnp.where(is_odd, QY - 1 - rest, rest)

    def interpolated(window, start):
        count = window.shape[0]
        here = pltpu.roll(window, lax.rem(count - start, count), 0)
        return near * here[:QY] + far * pltpu.roll(here, count - 1, 0)[:QY]

    row_y = lax.broadcasted_iota(jnp.int32, (QY, QZ), 0)

    def gradients(x):
        centre, minus, plus = ph[x + 1], ph[x], ph[x + 2]
        south_v = jnp.where(row_y == 0, yp[0, pl.ds(x, 1), :], pltpu.roll(centre, 1, 0))
        north_v = jnp.where(row_y == QY - 1, yp[1, pl.ds(x, 1), :], pltpu.roll(centre, QY - 1, 0))
        upper, lower = pltpu.roll(centre, QZ - 1, 1), pltpu.roll(centre, 1, 1)
        lap = (plus + minus) + (north_v + south_v) + (upper + lower) - 6.0 * centre
        mu = centre * (0.0625 * centre * centre - 0.0625) - 0.04 * lap
        half = 0.5 * mu
        mm[0] = mu
        mm[1] = half * (plus - minus)
        mm[2] = half * (north_v - south_v)
        mm[3] = half * (upper - lower)

    def collide_row(x, face):
        gradients(x)
        if face is not None:
            top = odd == face
            sign = jnp.where(top, 1.0, -1.0)
            jump = sign * (-plane_speed)

        def chunk(step, carry):
            zs = pl.ds(pl.multiple_of(step * 128, 128), 128)
            for h in range(2):
                rows = pl.ds(8 * h, 8)
                read = lambda ref, c: ref[c, x, rows, zs]
                f = [read(fin, c) for c in range(19)]
                phi = ph[x + 1, rows, zs]
                mu = mm[0, rows, zs]
                force = [mm[a, rows, zs] for a in (1, 2, 3)]
                diff = {c: f[c] - f[c + 1] for c in pairs}
                rho = f[0]
                for c in pairs:
                    rho = rho + (f[c] + f[c + 1])
                inverse = 1.0 / rho
                velocity = []
                for a in range(3):
                    total = 0.5 * force[a]
                    for c in pairs:
                        s = lattice_velocity[c][a]
                        if s:
                            total = total + diff[c] if s > 0 else total - diff[c]
                    velocity.append(total * inverse)
                ux, uy, uz = velocity
                u2 = ux * ux + uy * uy + uz * uz
                uf = ux * force[0] + uy * force[1] + uz * force[2]
                base = 1.25 * rho * (1.0 - 1.5 * u2) - 1.125 * uf
                scale = 5.625 * rho
                pull = [3.375 * part for part in force]
                gbase = (10.0 / 9.0) * (3.0 * mu - 1.5 * phi * u2)
                gscale = 5.0 * phi
                fin[0, x, rows, zs] = (1.0 / 3.0) * base - 0.25 * f[0]
                gin[0, x, rows, zs] = (10.0 / 9.0) * (phi - 2.0 * mu - 0.5 * phi * u2) - (
                    1.0 / 9.0
                ) * read(gin, 0)
                if face == 1:
                    common = -3.0 * uy - 1.5 * jump
                    wrho, wphi = jump * rho, jump * phi
                for c in pairs:
                    w = 1.0 / 18.0 if c < 7 else 1.0 / 36.0
                    direction = lattice_velocity[c]
                    p = axis_sum(direction, velocity)
                    b = axis_sum(direction, pull)
                    a = scale * p
                    ab = a + b
                    even = w * (base + p * ab)
                    oddpart = (w / 3.0) * (a + ab)
                    f_up = (even + oddpart) - 0.25 * f[c]
                    f_down = (even - oddpart) - 0.25 * f[c + 1]
                    h_p = gscale * p
                    geven = w * (gbase + p * h_p)
                    godd = (2.0 * w / 3.0) * h_p
                    g_up = (geven + godd) - (1.0 / 9.0) * read(gin, c)
                    g_down = (geven - godd) - (1.0 / 9.0) * read(gin, c + 1)
                    fin[c, x, rows, zs] = f_up
                    fin[c + 1, x, rows, zs] = f_down
                    gin[c, x, rows, zs] = g_up
                    gin[c + 1, x, rows, zs] = g_down
                    if face is not None and c in rising:
                        j = rising.index(c)
                        f_sent = jnp.where(top, f_up, f_down)
                        g_sent = jnp.where(top, g_up, g_down)
                        if face == 1:
                            cy = float(direction[1])
                            delta = common
                            if cy:
                                delta = delta + (cy * 9.0 * p + (cy * 3.0 * sign + 4.5 * jump))
                            f_sent = f_sent + w * (wrho * delta)
                            g_sent = g_sent + w * (wphi * delta)
                        sb[face, j, rows, zs] = f_sent
                        sb[face, 5 + j, rows, zs] = g_sent
            return carry

        lax.fori_loop(0, QZ // 128, chunk, 0)
        slot = jnp.where(top, 1, 0) if face is not None else x + 1
        group, line = slot // 4, lax.rem(slot, 4) * 10
        for d, chosen, y in ((0, northward, QY - 1), (1, southward, 0)):
            for j, c in enumerate(chosen):
                ys[d, group, pl.ds(line + j, 1), :] = fin[c, x, y : y + 1, :]
                ys[d, group, pl.ds(line + 5 + j, 1), :] = gin[c, x, y : y + 1, :]
        if face is not None:
            j_hi = jnp.where(top, 1, 2)
            for family in range(2):
                ce[face, 0, family : family + 1, :] = sb[face, j_hi + 5 * family, QY - 1 : QY, :]
                ce[face, 1, family : family + 1, :] = sb[face, 3 - j_hi + 5 * family, 0:1, :]

    def wait_f(x, carry):
        load(1, x).wait()
        return carry

    lax.fori_loop(0, QX, wait_f, 0)

    for copy in (phi_copies[0], phi_copies[3], phi_copies[4]):
        copy.wait_recv()
    collide_row(flat_x, 0)
    flat_copies = [
        remote(5, sb.at[0], ob, (flat_gx, gy)),
        remote(6, ce.at[0, 0], oc.at[0], (flat_gx, north)),
        remote(7, ce.at[0, 1], oc.at[1], (flat_gx, south)),
    ]
    for copy in flat_copies:
        copy.start()
    phi_copies[1].wait_recv()
    phi_copies[2].wait_recv()
    ph[9 * odd] = interpolated(wp[...], first)
    collide_row(plane_x, 1)
    plane_copies = [
        remote(8, ce.at[1, 0], we.at[0], (plane_gx, to_hi)),
        remote(9, ce.at[1, 1], we.at[1], (plane_gx, to_lo)),
        remote(10, sb.at[1], wb.at[:, pl.ds(8, QY)], (plane_gx, to_a)),
        remote(11, sb.at[1], wb.at[:, pl.ds(8 + QY, QY)], (plane_gx, to_b)),
    ]
    for copy in plane_copies:
        copy.start()

    def inner_row(x, carry):
        collide_row(x, None)
        return carry

    side_copies = [
        remote(12 + 2 * d + group, ys.at[d, group], yr.at[d, group], (gx, (north, south)[d]))
        for group in range(2)
        for d in range(2)
    ]
    lax.fori_loop(1, 3, inner_row, 0)
    side_copies[0].start()
    side_copies[1].start()
    lax.fori_loop(3, QX - 1, inner_row, 0)
    side_copies[2].start()
    side_copies[3].start()

    families = ((fin, fo), (gin, go))

    def stream_level(x, carry):
        for source, target in families:
            for c in level:
                target[c, x] = streamed(source[c, x], *lattice_velocity[c][1:])
        return carry

    def stream_across(x, carry):
        for source, target in families:
            for c in rising:
                _, step_y, step_z = lattice_velocity[c]
                target[c, x + 1] = streamed(source[c, x], step_y, step_z)
                target[c + 1, x] = streamed(source[c + 1, x + 1], -step_y, -step_z)
        return carry

    lax.fori_loop(0, QX, stream_level, 0)
    lax.fori_loop(0, QX - 1, stream_across, 0)

    for copy in side_copies:
        copy.wait_recv()

    def side_line(x):
        slot = jnp.where(x == 0, 0, jnp.where(x == QX - 1, 1, x + 1))
        return slot // 4, lax.rem(slot, 4) * 10

    def side_rows(x, chosen_x, shift):
        group, line = side_line(x)
        for d, chosen, y in ((0, northward, 0), (1, southward, QY - 1)):
            for j, c in enumerate(chosen):
                step_x, _, step_z = lattice_velocity[c]
                if step_x != chosen_x:
                    continue
                for family in range(2):
                    row = yr[d, group, pl.ds(line + 5 * family + j, 1), :]
                    if step_z:
                        row = pltpu.roll(row, step_z % QZ, 1)
                    families[family][1][c, x + shift, y : y + 1, :] = row

    def side_level(x, carry):
        side_rows(x, 0, 0)
        return carry

    def side_across(x, carry):
        side_rows(x, 1, 1)
        side_rows(x + 1, -1, -1)
        return carry

    lax.fori_loop(0, QX, side_level, 0)
    lax.fori_loop(0, QX - 1, side_across, 0)

    for copy in flat_copies:
        copy.wait_recv()

    def arrive_flat(sign, x):
        for j, c in enumerate(rising):
            step_y, step_z = sign * lattice_velocity[c][1], sign * lattice_velocity[c][2]
            c = c if sign > 0 else c + 1
            for family in range(2):
                v = streamed(ob[5 * family + j], step_y, step_z)
                if step_y > 0:
                    v = jnp.where(row_y == 0, oc[0, family : family + 1, :], v)
                elif step_y < 0:
                    v = jnp.where(row_y == QY - 1, oc[1, family : family + 1, :], v)
                families[family][1][c, x] = v

    pl.when(is_odd)(lambda: arrive_flat(1, 0))
    pl.when(jnp.logical_not(is_odd))(lambda: arrive_flat(-1, QX - 1))

    for copy in plane_copies:
        copy.wait_recv()

    def arrive_plane(sign, x):
        for j, c in enumerate(rising):
            step_y, step_z = sign * lattice_velocity[c][1], sign * lattice_velocity[c][2]
            c = c if sign > 0 else c + 1
            for family in range(2):
                k = 5 * family + j
                if step_y > 0:
                    wb[k, 7:8, :] = we[0, family : family + 1, :]
                elif step_y < 0:
                    wb[k, 8 + 2 * QY : 9 + 2 * QY, :] = we[1, family : family + 1, :]
                v = interpolated(wb[k], first + (8 - step_y))
                families[family][1][c, x] = streamed(v, 0, step_z)

    pl.when(jnp.logical_not(is_odd))(lambda: arrive_plane(1, 0))
    pl.when(is_odd)(lambda: arrive_plane(-1, QX - 1))

    for copy in phi_copies + flat_copies + plane_copies + side_copies:
        copy.wait_send()


def on_device(momentum_dist, order_dist, offsets):
    block = (19, QX, QY, QZ)
    f32 = jnp.float32
    vmem = pl.BlockSpec(memory_space=pltpu.VMEM)
    return pl.pallas_call(
        step_kernel,
        out_shape=(pltpu.VMEM(block, f32), pltpu.VMEM(block, f32)),
        in_specs=[
            pl.BlockSpec(memory_space=pltpu.SMEM),
            pl.BlockSpec(memory_space=pltpu.HBM),
            pl.BlockSpec(memory_space=pltpu.HBM),
        ],
        out_specs=(vmem, vmem),
        scratch_shapes=[
            pltpu.VMEM(block, f32),
            pltpu.VMEM(block, f32),
            pltpu.VMEM((QX + 2, QY, QZ), f32),
            pltpu.VMEM((2 * QY, QZ), f32),
            pltpu.VMEM((2, QX, QZ), f32),
            pltpu.VMEM((2, QX, QZ), f32),
            pltpu.VMEM((4, QY, QZ), f32),
            pltpu.VMEM((2, 10, QY, QZ), f32),
            pltpu.VMEM((10, QY, QZ), f32),
            pltpu.VMEM((2, 8, QZ), f32),
            pltpu.VMEM((10, 2 * QY + 16, QZ), f32),
            pltpu.VMEM((2, 8, QZ), f32),
            pltpu.VMEM((2, 2, 8, QZ), f32),
            pltpu.VMEM((2, 2, 40, QZ), f32),
            pltpu.VMEM((2, 2, 40, QZ), f32),
            pltpu.SemaphoreType.DMA((2, QX)),
            pltpu.SemaphoreType.DMA((16,)),
            pltpu.SemaphoreType.DMA((16,)),
        ],
        compiler_params=pltpu.CompilerParams(
            collective_id=0, has_side_effects=True, vmem_limit_bytes=40 * 2**20
        ),
    )(
        offsets,
        pltpu.with_memory_space_constraint(momentum_dist, pltpu.HBM),
        pltpu.with_memory_space_constraint(order_dist, pltpu.HBM),
    )


def solution(mesh):
    return jax.shard_map(
        on_device,
        mesh=mesh,
        in_specs=(P(None, "gx", "gy", None), P(None, "gx", "gy", None), P()),
        out_specs=(P(None, "gx", "gy", None), P(None, "gx", "gy", None)),
        check_vma=False,
    )
```

time: 272 us -> 49.4 us (0.18)
  waiting for transfers between devices: 67.6 us -> 0 us
  other arithmetic: 50 us -> 0 us
  local copies, waits for them, and re-layouts: 53.7 us -> 5.19 us
  Pallas kernels: 0 us -> 43.4 us
  blocking collectives: 41.7 us -> 0 us
  starting transfers between devices: 38.4 us -> 0 us
  between operations: 19.8 us -> 0.65 us
    ppermute x8 -> x0, waiting for transfers between devices: 56.4 us -> none  [the longest x4 32.6 us: extended(): lax.ppermute(tail, axis, [(i, (i + 1) % count) for i in range(count)])]
    pallas_call x0 -> x1, Pallas kernels: none -> 43.4 us  [on_device(): pl.pallas_call(step_kernel, out_shape=(pltpu.VMEM(block, f32), pltpu.VMEM...]
    all_gather x2 -> x0, blocking collectives: 41.7 us -> none  [the longest x1 23.2 us: plane_windows(): lax.all_gather(up_piece, 'gy', axis=1, tiled=True)]
    ppermute x8 -> x0, starting transfers between devices: 38.3 us -> none  [the longest x4 26.1 us: extended(): lax.ppermute(tail, axis, [(i, (i + 1) % count) for i in range(count)])]
    slice x40 -> x0, local copies, waits for them, and re-layouts: 25.7 us -> none  [the longest x22 13.5 us: stream(): arrived_list.append(jnp.roll(shifted, step_z, 2))]
    unnamed x34 -> x0, other arithmetic: 15.2 us -> none
    unnamed x223 -> x4, local copies, waits for them, and re-layouts: 18.9 us -> 5.19 us
    reduce_sum x4 -> x0, other arithmetic: 12.4 us -> none  [the longest x1 3.61 us: collide(): jnp.sum(directions[axis_place] * momentum, axis=0)]
  transfers between devices with their start and end apart: 10 -> 0, of which waited for: 4 -> 0; matrix products, arithmetic and copies ran while one was open for 18% -> 0% of each run, Pallas kernels for 0% -> 0%
where the time goes in v1:
time: 49.4 us; the launch traced here: 49.3 us
  Pallas kernels  43.4 us (88%)
  local copies, waits for them, and re-layouts  5.19 us (11%)
  between operations  0.65 us (1%)
    pallas_call x1, Pallas kernels, on_device(): pl.pallas_call(step_kernel, out_shape=(pltpu.VMEM(block, f32), pltpu.VMEM...  43.4 us
    unnamed x4, local copies, waits for them, and re-layouts  5.19 us

profile of v1, /device:TPU:1, one launch (start us, length us, event | category | flops | bytes accessed | tf_op | source)
XLA Modules:
  0.0 49.3 jit_solution(15935877014039271307)
XLA Ops:
  0.6 0.0 copy-start
  0.6 0.6 %copy-done = s32[4]{0:T(128)S(1)} copy-done((s32[4]{0:T(128)S(1)}, s32[4]{0:T(128)}, u32[]{:S(2)}) %copy-start) | copy-done | bytes 40
  1.3 43.4 %shard_map.50 = (f32[19,8,16,512]{3,2,1,0:T(8,128)S(1)}, f32[19,8,16,512]{3,2,1,0:T(8,128)S(1)}) custom-call(s32[4]{0:T(128)S(1)} %copy-done, f32[19,8,16,512]{3,2,1,0:T(8,128)} %f_hbm.1, f32[19,8,16,512]{3,2,1,0:T(8,128)} %g_hbm.1), custom_call_target="tpu_custom_call" | custom-call | tf_op jit(solution)/shard_map/pallas_call | solution.py:381
  44.7 2.3 %copy.7 = f32[19,8,16,512]{3,2,1,0:T(8,128)} copy(f32[19,8,16,512]{3,2,1,0:T(8,128)S(1)} %get-tuple-element.2) | data formatting | bytes 9961472
  47.0 2.3 %copy.8 = f32[19,8,16,512]{3,2,1,0:T(8,128)} copy(f32[19,8,16,512]{3,2,1,0:T(8,128)S(1)} %get-tuple-element.3) | data formatting | bytes 9961472
Async XLA Ops:
  0.6 0.7 %copy-start = (s32[4]{0:T(128)S(1)}, s32[4]{0:T(128)}, u32[]{:S(2)}) copy-start(s32[4]{0:T(128)} %off_ref.1) | copy-start | bytes 52

commit v2 on v1

--- a/solution.py
+++ b/solution.py
@@ -58,9 +58,9 @@
 
 
 def step_kernel(
-    off_ref, f_hbm, g_hbm, fo, go,
-    fin, gin, ph, wp, yps, yp, mm, sb, ob, oc, wb, we, ce, ys, yr,
-    load_sem, send_sem, recv_sem,
+    off_hbm, f_hbm, g_hbm, fo, go,
+    off_ref, fin, gin, ph, wp, yps, yp, mm, sb, ob, oc, wb, we, ce, ys, yr,
+    load_sem, off_sem, send_sem, recv_sem,
 ):
     gx, gy = lax.axis_index("gx"), lax.axis_index("gy")
     odd = lax.rem(gx, 2)
@@ -69,12 +69,14 @@
     plane_gx = lax.rem(gx + 2 * odd + NGX - 1, NGX)
     ring = lambda v: lax.rem(v + 2 * NGY, NGY)
     north, south = ring(gy + 1), ring(gy - 1)
-    to_a, to_b = ring(gy + 9 - 17 * odd), ring(gy + 8 - 17 * odd)
+    main_gy, extra_gy = ring(gy + 8), ring(gy + 9 - 18 * odd)
+    core_gy = gy + 1 - 2 * lax.rem(gy, 2)
+    sends_twice = lax.rem(gx + gy, 2) == 1
     to_hi, to_lo = ring(gy + 10 - 17 * odd), ring(gy + 7 - 17 * odd)
     partners = [
         (gx, north), (gx, south),
         (flat_gx, gy), (flat_gx, north), (flat_gx, south),
-        (plane_gx, to_a), (plane_gx, to_b), (plane_gx, to_hi), (plane_gx, to_lo),
+        (plane_gx, main_gy), (plane_gx, extra_gy), (plane_gx, to_hi), (plane_gx, to_lo),
     ]
     barrier = pltpu.get_barrier_semaphore()
     for partner in partners:
@@ -85,8 +87,10 @@
         return pltpu.make_async_copy(source.at[:, x], target.at[:, x], load_sem.at[which, x])
 
     for which in range(2):
-        for x in range(QX):
+        for x in (0, QX - 1, *range(1, QX - 1)):
             load(which, x).start()
+    load_offsets = pltpu.make_async_copy(off_hbm, off_ref, off_sem)
+    load_offsets.start()
 
     def remote(k, source, target, device):
         return pltpu.make_async_remote_copy(
@@ -104,20 +108,25 @@
         yps[1, pl.ds(x, 1), :] = total[0:1]
         return carry
 
-    lax.fori_loop(0, QX, phi_row, 0)
-
+    phi_row(0, 0)
+    phi_row(QX - 1, 0)
     flat_x, plane_x = 7 - 7 * odd, 7 * odd
+    main_slot = 1 - odd
     phi_copies = [
         remote(0, ph.at[flat_x + 1], ph.at[9 * odd], (flat_gx, gy)),
-        remote(1, ph.at[plane_x + 1], wp.at[pl.ds(0, QY)], (plane_gx, to_a)),
-        remote(2, ph.at[plane_x + 1], wp.at[pl.ds(QY, QY)], (plane_gx, to_b)),
+        remote(1, ph.at[plane_x + 1], wp.at[main_slot], (plane_gx, main_gy)),
+        remote(2, ph.at[plane_x + 1], wp.at[1 - main_slot], (plane_gx, extra_gy)),
         remote(3, yps.at[0], yp.at[0], (gx, north)),
         remote(4, yps.at[1], yp.at[1], (gx, south)),
     ]
     pl.semaphore_wait(barrier, len(partners))
-    for copy in phi_copies:
+    for copy in phi_copies[:3]:
         copy.start()
-
+    lax.fori_loop(1, QX - 1, phi_row, 0)
+    for copy in phi_copies[3:]:
+        copy.start()
+
+    load_offsets.wait()
     plane = lax.rem((gx + odd) // 2, 4)
     fraction = (2 * plane + 1).astype(jnp.float32) * 0.125
     near = jnp.where(is_odd, fraction, 1.0 - fraction)
@@ -255,16 +264,37 @@
         copy.start()
     phi_copies[1].wait_recv()
     phi_copies[2].wait_recv()
-    ph[9 * odd] = interpolated(wp[...], first)
+    ph[9 * odd] = interpolated(wp[...].reshape(2 * QY, QZ), first)
     collide_row(plane_x, 1)
     plane_copies = [
         remote(8, ce.at[1, 0], we.at[0], (plane_gx, to_hi)),
         remote(9, ce.at[1, 1], we.at[1], (plane_gx, to_lo)),
-        remote(10, sb.at[1], wb.at[:, pl.ds(8, QY)], (plane_gx, to_a)),
-        remote(11, sb.at[1], wb.at[:, pl.ds(8 + QY, QY)], (plane_gx, to_b)),
-    ]
-    for copy in plane_copies:
+    ]
+    rows_at = lambda half, slot: wb.at[pl.ds(5 * half, 5), pl.ds(8 + QY * slot, QY)]
+    layer = lambda half: sb.at[1, pl.ds(5 * half, 5)]
+    main_copies = [
+        remote(10 + half, layer(half), rows_at(half, main_slot), (plane_gx, main_gy))
+        for half in range(2)
+    ]
+    extra_copies = [
+        remote(16 + half, layer(half), rows_at(half, 1 - main_slot), (plane_gx, extra_gy))
+        for half in range(2)
+    ]
+    hand_on = [
+        pltpu.make_async_remote_copy(
+            src_ref=rows_at(half, odd), dst_ref=rows_at(half, 1 - odd),
+            send_sem=send_sem.at[18 + half], recv_sem=recv_sem.at[16 + half],
+            device_id=(gx, core_gy), device_id_type=MESH,
+        )
+        for half in range(2)
+    ]
+    for copy in plane_copies + main_copies:
         copy.start()
+
+    @pl.when(sends_twice)
+    def _():
+        for copy in extra_copies:
+            copy.start()
 
     def inner_row(x, carry):
         collide_row(x, None)
@@ -351,7 +381,10 @@
     pl.when(is_odd)(lambda: arrive_flat(1, 0))
     pl.when(jnp.logical_not(is_odd))(lambda: arrive_flat(-1, QX - 1))
 
-    for copy in plane_copies:
+    for half in range(2):
+        main_copies[half].wait_recv()
+        pl.when(sends_twice)(hand_on[half].start)
+    for copy in plane_copies + extra_copies:
         copy.wait_recv()
 
     def arrive_plane(sign, x):
@@ -370,50 +403,78 @@
     pl.when(jnp.logical_not(is_odd))(lambda: arrive_plane(1, 0))
     pl.when(is_odd)(lambda: arrive_plane(-1, QX - 1))
 
-    for copy in phi_copies + flat_copies + plane_copies + side_copies:
+    for copy in phi_copies + flat_copies + plane_copies + main_copies + side_copies:
         copy.wait_send()
+
+    @pl.when(sends_twice)
+    def _():
+        for copy in extra_copies + hand_on:
+            copy.wait_send()
+
+
+def write_kernel(f, g, f_hbm, g_hbm, sem):
+    copies = [
+        pltpu.make_async_copy(source.at[:, x], target.at[:, x], sem.at[which, x])
+        for x in range(QX)
+        for which, (source, target) in enumerate(((f, f_hbm), (g, g_hbm)))
+    ]
+    for copy in copies:
+        copy.start()
+    for copy in copies:
+        copy.wait()
 
 
 def on_device(momentum_dist, order_dist, offsets):
     block = (19, QX, QY, QZ)
     f32 = jnp.float32
-    vmem = pl.BlockSpec(memory_space=pltpu.VMEM)
-    return pl.pallas_call(
+    vmem, hbm = pl.BlockSpec(memory_space=pltpu.VMEM), pl.BlockSpec(memory_space=pltpu.HBM)
+    f_new, g_new = pl.pallas_call(
         step_kernel,
         out_shape=(pltpu.VMEM(block, f32), pltpu.VMEM(block, f32)),
-        in_specs=[
-            pl.BlockSpec(memory_space=pltpu.SMEM),
-            pl.BlockSpec(memory_space=pltpu.HBM),
-            pl.BlockSpec(memory_space=pltpu.HBM),
-        ],
+        in_specs=[hbm, hbm, hbm],
         out_specs=(vmem, vmem),
         scratch_shapes=[
+            pltpu.SMEM((4,), jnp.int32),
             pltpu.VMEM(block, f32),
             pltpu.VMEM(block, f32),
             pltpu.VMEM((QX + 2, QY, QZ), f32),
-            pltpu.VMEM((2 * QY, QZ), f32),
+            pltpu.VMEM((2, QY, QZ), f32),
             pltpu.VMEM((2, QX, QZ), f32),
             pltpu.VMEM((2, QX, QZ), f32),
             pltpu.VMEM((4, QY, QZ), f32),
             pltpu.VMEM((2, 10, QY, QZ), f32),
             pltpu.VMEM((10, QY, QZ), f32),
-            pltpu.VMEM((2, 8, QZ), f32),
+            pltpu.VMEM((2, 2, QZ), f32),
             pltpu.VMEM((10, 2 * QY + 16, QZ), f32),
-            pltpu.VMEM((2, 8, QZ), f32),
-            pltpu.VMEM((2, 2, 8, QZ), f32),
+            pltpu.VMEM((2, 2, QZ), f32),
+            pltpu.VMEM((2, 2, 2, QZ), f32),
             pltpu.VMEM((2, 2, 40, QZ), f32),
             pltpu.VMEM((2, 2, 40, QZ), f32),
             pltpu.SemaphoreType.DMA((2, QX)),
-            pltpu.SemaphoreType.DMA((16,)),
-            pltpu.SemaphoreType.DMA((16,)),
+            pltpu.SemaphoreType.DMA,
+            pltpu.SemaphoreType.DMA((20,)),
+            pltpu.SemaphoreType.DMA((18,)),
         ],
         compiler_params=pltpu.CompilerParams(
-            collective_id=0, has_side_effects=True, vmem_limit_bytes=40 * 2**20
+            collective_id=0, has_side_effects=True, vmem_limit_bytes=32 * 2**20
         ),
     )(
-        offsets,
-        pltpu.with_memory_space_constraint(momentum_dist, pltpu.HBM),
-        pltpu.with_memory_space_constraint(order_dist, pltpu.HBM),
+        *(
+            pltpu.with_memory_space_constraint(operand, pltpu.HBM)
+            for operand in (offsets, momentum_dist, order_dist)
+        )
+    )
+    whole = jax.ShapeDtypeStruct(block, f32)
+    return pl.pallas_call(
+        write_kernel,
+        out_shape=(whole, whole),
+        in_specs=[vmem, vmem],
+        out_specs=(hbm, hbm),
+        scratch_shapes=[pltpu.SemaphoreType.DMA((2, QX))],
+        compiler_params=pltpu.CompilerParams(vmem_limit_bytes=4 * 2**20),
+    )(
+        pltpu.with_memory_space_constraint(f_new, pltpu.VMEM),
+        pltpu.with_memory_space_constraint(g_new, pltpu.VMEM),
     )
 
 

time: 49.4 us -> 44.4 us (0.90)
  local copies, waits for them, and re-layouts: 5.19 us -> 0 us
    unnamed x4 -> x0, local copies, waits for them, and re-layouts: 5.19 us -> none
    pallas_call x0 -> x1, Pallas kernels: none -> 3.9 us  [on_device(): pl.pallas_call(write_kernel, out_shape=(whole, whole), in_specs=[vmem, vm...]
    pallas_call x1, Pallas kernels: 43.4 us -> 39.7 us  [on_device(): pl.pallas_call(step_kernel, out_shape=(pltpu.VMEM(block, f32), pltpu.VMEM...]
where the time goes in v2:
time: 44.4 us; the launch traced here: 44.2 us
  Pallas kernels  43.6 us (98%)
  between operations  0.64 us (1%)
    pallas_call x1, Pallas kernels, on_device(): pl.pallas_call(step_kernel, out_shape=(pltpu.VMEM(block, f32), pltpu.VMEM...  39.7 us
    pallas_call x1, Pallas kernels, on_device(): pl.pallas_call(write_kernel, out_shape=(whole, whole), in_specs=[vmem, vm...  3.9 us

profile of v2, /device:TPU:1, one launch (start us, length us, event | category | flops | bytes accessed | tf_op | source)
XLA Modules:
  0.0 44.2 jit_solution(10754304352677417493)
XLA Ops:
  0.6 39.7 %shard_map.50 = (f32[19,8,16,512]{3,2,1,0:T(8,128)S(1)}, f32[19,8,16,512]{3,2,1,0:T(8,128)S(1)}) custom-call(s32[4]{0:T(128)} %off_hbm.1, f32[19,8,16,512]{3,2,1,0:T(8,128)} %f_hbm.1, f32[19,8,16,512]{3,2,1,0:T(8,128)} %g_hbm.1), custom_call_target="tpu_custom_call" | custom-call | tf_op jit(solution)/shard_map/pallas_call | solution.py:431
  40.3 3.9 %shard_map.51 = (f32[19,8,16,512]{3,2,1,0:T(8,128)}, f32[19,8,16,512]{3,2,1,0:T(8,128)}) custom-call(f32[19,8,16,512]{3,2,1,0:T(8,128)S(1)} %get-tuple-element.4.f, f32[19,8,16,512]{3,2,1,0:T(8,128)S(1)} %get-tuple-element.5.g), custom_call_target="tpu_custom_call" | custom-call | tf_op jit(solution)/shard_map/pallas_call | solution.py:468

commit v3 on v2

--- a/solution.py
+++ b/solution.py
@@ -120,7 +120,7 @@
         remote(4, yps.at[1], yp.at[1], (gx, south)),
     ]
     pl.semaphore_wait(barrier, len(partners))
-    for copy in phi_copies[:3]:
+    for copy in (phi_copies[1], phi_copies[2], phi_copies[0]):
         copy.start()
     lax.fori_loop(1, QX - 1, phi_row, 0)
     for copy in phi_copies[3:]:
@@ -256,7 +256,7 @@
         copy.wait_recv()
     collide_row(flat_x, 0)
     flat_copies = [
-        remote(5, sb.at[0], ob, (flat_gx, gy)),
+        remote(5, sb.at[0, pl.ds(0, 4)], ob.at[pl.ds(0, 4)], (flat_gx, gy)),
         remote(6, ce.at[0, 0], oc.at[0], (flat_gx, north)),
         remote(7, ce.at[0, 1], oc.at[1], (flat_gx, south)),
     ]
@@ -283,7 +283,7 @@
     hand_on = [
         pltpu.make_async_remote_copy(
             src_ref=rows_at(half, odd), dst_ref=rows_at(half, 1 - odd),
-            send_sem=send_sem.at[18 + half], recv_sem=recv_sem.at[16 + half],
+            send_sem=send_sem.at[19 + half], recv_sem=recv_sem.at[16 + half],
             device_id=(gx, core_gy), device_id_type=MESH,
         )
         for half in range(2)
@@ -329,6 +329,8 @@
         return carry
 
     lax.fori_loop(0, QX, stream_level, 0)
+    flat_copies.append(remote(18, sb.at[0, pl.ds(4, 6)], ob.at[pl.ds(4, 6)], (flat_gx, gy)))
+    flat_copies[-1].start()
     lax.fori_loop(0, QX - 1, stream_across, 0)
 
     for copy in side_copies:
@@ -452,8 +454,8 @@
             pltpu.VMEM((2, 2, 40, QZ), f32),
             pltpu.SemaphoreType.DMA((2, QX)),
             pltpu.SemaphoreType.DMA,
-            pltpu.SemaphoreType.DMA((20,)),
-            pltpu.SemaphoreType.DMA((18,)),
+            pltpu.SemaphoreType.DMA((21,)),
+            pltpu.SemaphoreType.DMA((19,)),
         ],
         compiler_params=pltpu.CompilerParams(
             collective_id=0, has_side_effects=True, vmem_limit_bytes=32 * 2**20

time: 44.4 us -> 40.9 us (0.921)
  Pallas kernels: 43.6 us -> 39.7 us
    pallas_call x1, Pallas kernels: 39.7 us -> 35.8 us  [on_device(): pl.pallas_call(step_kernel, out_shape=(pltpu.VMEM(block, f32), pltpu.VMEM...]
where the time goes in v3:
time: 40.9 us; the launch traced here: 40.3 us
  Pallas kernels  39.7 us (97%)
  between operations  0.64 us (2%)
    pallas_call x1, Pallas kernels, on_device(): pl.pallas_call(step_kernel, out_shape=(pltpu.VMEM(block, f32), pltpu.VMEM...  35.8 us
    pallas_call x1, Pallas kernels, on_device(): pl.pallas_call(write_kernel, out_shape=(whole, whole), in_specs=[vmem, vm...  3.9 us

profile of v3, /device:TPU:1, one launch (start us, length us, event | category | flops | bytes accessed | tf_op | source)
XLA Modules:
  0.0 40.3 jit_solution(4577782930215527189)
XLA Ops:
  0.6 35.8 %shard_map.50 = (f32[19,8,16,512]{3,2,1,0:T(8,128)S(1)}, f32[19,8,16,512]{3,2,1,0:T(8,128)S(1)}) custom-call(s32[4]{0:T(128)} %off_hbm.1, f32[19,8,16,512]{3,2,1,0:T(8,128)} %f_hbm.1, f32[19,8,16,512]{3,2,1,0:T(8,128)} %g_hbm.1), custom_call_target="tpu_custom_call" | custom-call | tf_op jit(solution)/shard_map/pallas_call | solution.py:433
  36.4 3.9 %shard_map.51 = (f32[19,8,16,512]{3,2,1,0:T(8,128)}, f32[19,8,16,512]{3,2,1,0:T(8,128)}) custom-call(f32[19,8,16,512]{3,2,1,0:T(8,128)S(1)} %get-tuple-element.4.f, f32[19,8,16,512]{3,2,1,0:T(8,128)S(1)} %get-tuple-element.5.g), custom_call_target="tpu_custom_call" | custom-call | tf_op jit(solution)/shard_map/pallas_call | solution.py:470

commit v4 on v3

--- a/solution.py
+++ b/solution.py
@@ -365,6 +365,10 @@
     lax.fori_loop(0, QX, side_level, 0)
     lax.fori_loop(0, QX - 1, side_across, 0)
 
+    for half in range(2):
+        main_copies[half].wait_recv()
+        pl.when(sends_twice)(hand_on[half].start)
+
     for copy in flat_copies:
         copy.wait_recv()
 
@@ -383,9 +387,6 @@
     pl.when(is_odd)(lambda: arrive_flat(1, 0))
     pl.when(jnp.logical_not(is_odd))(lambda: arrive_flat(-1, QX - 1))
 
-    for half in range(2):
-        main_copies[half].wait_recv()
-        pl.when(sends_twice)(hand_on[half].start)
     for copy in plane_copies + extra_copies:
         copy.wait_recv()
 

time: 40.9 us -> 40 us (0.978); the launches traced: 40.3 us -> 39.8 us
  Pallas kernels: 39.7 us -> 39.2 us
    pallas_call x1, Pallas kernels: 35.8 us -> 35.3 us  [on_device(): pl.pallas_call(step_kernel, out_shape=(pltpu.VMEM(block, f32), pltpu.VMEM...]
where the time goes in v4:
time: 40 us; the launch traced here: 39.8 us
  Pallas kernels  39.2 us (98%)
  between operations  0.64 us (2%)
    pallas_call x1, Pallas kernels, on_device(): pl.pallas_call(step_kernel, out_shape=(pltpu.VMEM(block, f32), pltpu.VMEM...  35.3 us
    pallas_call x1, Pallas kernels, on_device(): pl.pallas_call(write_kernel, out_shape=(whole, whole), in_specs=[vmem, vm...  3.9 us

profile of v4, /device:TPU:1, one launch (start us, length us, event | category | flops | bytes accessed | tf_op | source)
XLA Modules:
  0.0 39.8 jit_solution(10321718231395757150)
XLA Ops:
  0.6 35.3 %shard_map.50 = (f32[19,8,16,512]{3,2,1,0:T(8,128)S(1)}, f32[19,8,16,512]{3,2,1,0:T(8,128)S(1)}) custom-call(s32[4]{0:T(128)} %off_hbm.1, f32[19,8,16,512]{3,2,1,0:T(8,128)} %f_hbm.1, f32[19,8,16,512]{3,2,1,0:T(8,128)} %g_hbm.1), custom_call_target="tpu_custom_call" | custom-call | tf_op jit(solution)/shard_map/pallas_call | solution.py:434
  35.9 3.9 %shard_map.51 = (f32[19,8,16,512]{3,2,1,0:T(8,128)}, f32[19,8,16,512]{3,2,1,0:T(8,128)}) custom-call(f32[19,8,16,512]{3,2,1,0:T(8,128)S(1)} %get-tuple-element.4.f, f32[19,8,16,512]{3,2,1,0:T(8,128)S(1)} %get-tuple-element.5.g), custom_call_target="tpu_custom_call" | custom-call | tf_op jit(solution)/shard_map/pallas_call | solution.py:471

commit v5 on v4

--- a/solution.py
+++ b/solution.py
@@ -262,6 +262,11 @@
     ]
     for copy in flat_copies:
         copy.start()
+    def inner_row(x, carry):
+        collide_row(x, None)
+        return carry
+
+    lax.fori_loop(1, 3, inner_row, 0)
     phi_copies[1].wait_recv()
     phi_copies[2].wait_recv()
     ph[9 * odd] = interpolated(wp[...].reshape(2 * QY, QZ), first)
@@ -296,16 +301,11 @@
         for copy in extra_copies:
             copy.start()
 
-    def inner_row(x, carry):
-        collide_row(x, None)
-        return carry
-
     side_copies = [
         remote(12 + 2 * d + group, ys.at[d, group], yr.at[d, group], (gx, (north, south)[d]))
         for group in range(2)
         for d in range(2)
     ]
-    lax.fori_loop(1, 3, inner_row, 0)
     side_copies[0].start()
     side_copies[1].start()
     lax.fori_loop(3, QX - 1, inner_row, 0)

time: 40 us -> 40.2 us (level)
  no operation moved by 1% of the time
where the time goes in v5:
time: 40.2 us; the launch traced here: 40 us
  Pallas kernels  39.4 us (98%)
  between operations  0.64 us (2%)
    pallas_call x1, Pallas kernels, on_device(): pl.pallas_call(step_kernel, out_shape=(pltpu.VMEM(block, f32), pltpu.VMEM...  35.5 us
    pallas_call x1, Pallas kernels, on_device(): pl.pallas_call(write_kernel, out_shape=(whole, whole), in_specs=[vmem, vm...  3.9 us

profile of v5, /device:TPU:1, one launch (start us, length us, event | category | flops | bytes accessed | tf_op | source)
XLA Modules:
  0.0 40.0 jit_solution(16981289746417853367)
XLA Ops:
  0.6 35.5 %shard_map.50 = (f32[19,8,16,512]{3,2,1,0:T(8,128)S(1)}, f32[19,8,16,512]{3,2,1,0:T(8,128)S(1)}) custom-call(s32[4]{0:T(128)} %off_hbm.1, f32[19,8,16,512]{3,2,1,0:T(8,128)} %f_hbm.1, f32[19,8,16,512]{3,2,1,0:T(8,128)} %g_hbm.1), custom_call_target="tpu_custom_call" | custom-call | tf_op jit(solution)/shard_map/pallas_call | solution.py:434
  36.1 3.9 %shard_map.51 = (f32[19,8,16,512]{3,2,1,0:T(8,128)}, f32[19,8,16,512]{3,2,1,0:T(8,128)}) custom-call(f32[19,8,16,512]{3,2,1,0:T(8,128)S(1)} %get-tuple-element.4.f, f32[19,8,16,512]{3,2,1,0:T(8,128)S(1)} %get-tuple-element.5.g), custom_call_target="tpu_custom_call" | custom-call | tf_op jit(solution)/shard_map/pallas_call | solution.py:471

commit v6 on v4

--- a/solution.py
+++ b/solution.py
@@ -328,9 +328,9 @@
                 target[c + 1, x] = streamed(source[c + 1, x + 1], -step_y, -step_z)
         return carry
 
-    lax.fori_loop(0, QX, stream_level, 0)
     flat_copies.append(remote(18, sb.at[0, pl.ds(4, 6)], ob.at[pl.ds(4, 6)], (flat_gx, gy)))
     flat_copies[-1].start()
+    lax.fori_loop(0, QX, stream_level, 0)
     lax.fori_loop(0, QX - 1, stream_across, 0)
 
     for copy in side_copies:

time: 40 us -> 40 us (level)
  no operation moved by 1% of the time
where the time goes in v6:
time: 40 us; the launch traced here: 39.8 us
  Pallas kernels  39.2 us (98%)
  between operations  0.64 us (2%)
    pallas_call x1, Pallas kernels, on_device(): pl.pallas_call(step_kernel, out_shape=(pltpu.VMEM(block, f32), pltpu.VMEM...  35.3 us
    pallas_call x1, Pallas kernels, on_device(): pl.pallas_call(write_kernel, out_shape=(whole, whole), in_specs=[vmem, vm...  3.9 us

profile of v6, /device:TPU:1, one launch (start us, length us, event | category | flops | bytes accessed | tf_op | source)
XLA Modules:
  0.0 39.8 jit_solution(16556283530281410684)
XLA Ops:
  0.6 35.3 %shard_map.50 = (f32[19,8,16,512]{3,2,1,0:T(8,128)S(1)}, f32[19,8,16,512]{3,2,1,0:T(8,128)S(1)}) custom-call(s32[4]{0:T(128)} %off_hbm.1, f32[19,8,16,512]{3,2,1,0:T(8,128)} %f_hbm.1, f32[19,8,16,512]{3,2,1,0:T(8,128)} %g_hbm.1), custom_call_target="tpu_custom_call" | custom-call | tf_op jit(solution)/shard_map/pallas_call | solution.py:434
  35.9 3.9 %shard_map.51 = (f32[19,8,16,512]{3,2,1,0:T(8,128)}, f32[19,8,16,512]{3,2,1,0:T(8,128)}) custom-call(f32[19,8,16,512]{3,2,1,0:T(8,128)S(1)} %get-tuple-element.4.f, f32[19,8,16,512]{3,2,1,0:T(8,128)S(1)} %get-tuple-element.5.g), custom_call_target="tpu_custom_call" | custom-call | tf_op jit(solution)/shard_map/pallas_call | solution.py:471
